TPU v7x, 512 devices: a whole 4x8x8 slice. The times are simulated.
512 devices in a mesh: dp: 32 (over z, y_hi, core), group: 16 (over y_lo, x).
Axes of the slice: x: 4, y: 8 (y_hi: 2, y_lo: 4; y = y_hi * 4 + y_lo), z: 8, core: 2. Of those that a mesh axis runs over, the one named last changes fastest.
Arguments:
- activations: bfloat16 [131072, 4096], P(('dp', 'group'))
- cotangent: bfloat16 [131072, 4096], P(('dp', 'group'))
- user_ids: int32 [512], P(('dp', 'group')), may hold values from 0 to 1, as said below
- adapters: bfloat16 [2, 2, 16, 4096], replicated, may hold values from -0.09375 to 0.09375
- clip_norm_ratio: float32 [1], replicated, may hold values from 3 to 5.5
Outputs:
- clipped_sum: float32 [2, 2, 16, 4096], P(None, None, None, 'group')
Inputs may be any that keep to these rules, and one draw needn't show every extreme that they name: `user_ids`: each consecutive block of 16 sequences is one user group in which every user number names exactly 8 sequences.
All inputs are finite; a program needn't handle non-finite values.
Results may differ from a plain program's by a relative error of at most 0.0021.
Values sent between devices are 32-bit elements; how exact they have to be, the bound alone decides.
No kernel may reach another device: no remote copies, remote signals or barrier semaphores. Data moves between devices by JAX's collectives and lax.ppermute only.
A program may use at most 64 MiB of HBM per device.

v0:
```python
import math

import jax
import jax.numpy as jnp
from jax import lax
from jax.sharding import PartitionSpec as P

GROUP_USERS = 2


adapter_scale = 2.0


def project(input_batch, matrix):
    return jnp.einsum("td,rd->tr", input_batch, matrix, preferred_element_type=jnp.float32)


def expand_rows(small_matrix, matrix):
    return jnp.dot(small_matrix, matrix, preferred_element_type=jnp.float32)


def user_grads(small_matrix, input_batch, token_owner):
    count = small_matrix.shape[0]
    masked = (small_matrix[:, None, :] * token_owner[:, :, None]).reshape(
        count, GROUP_USERS * small_matrix.shape[1]
    )
    summed_gradient = jnp.einsum(
        "tk,td->kd", masked, input_batch, preferred_element_type=jnp.float32
    )
    return (adapter_scale * summed_gradient).reshape(
        GROUP_USERS, small_matrix.shape[1], input_batch.shape[1]
    )


def on_device(activations, cotangent, user_ids, adapters, clip_norm_ratio):
    token_count, model_width = activations.shape
    seq_count = user_ids.shape[0]
    sequence_length = token_count // seq_count
    adapter_rank = adapters.shape[2]
    group_size = lax.axis_size("group")
    user_sequences = seq_count * group_size // GROUP_USERS
    seq_owner = (user_ids[:, None] == jnp.arange(GROUP_USERS, dtype=jnp.int32)[None, :]).astype(
        jnp.bfloat16
    )
    token_owner = jnp.broadcast_to(
        seq_owner[:, None, :], (seq_count, sequence_length, GROUP_USERS)
    ).reshape(token_count, GROUP_USERS)
    down_first = adapters[0, 0]
    first_up_weight = adapters[0, 1]
    second_down_weight = adapters[1, 0]
    up_second = adapters[1, 1]
    first_inner_state = project(activations, down_first).astype(jnp.bfloat16)
    hidden_state = (
        activations.astype(jnp.float32)
        + adapter_scale * expand_rows(first_inner_state, first_up_weight)
    ).astype(jnp.bfloat16)
    inner_second = project(hidden_state, second_down_weight).astype(jnp.bfloat16)
    second_cotangent = project(cotangent, up_second).astype(jnp.bfloat16)
    grads_second = jnp.stack(
        [
            user_grads(second_cotangent, hidden_state, token_owner),
            user_grads(inner_second, cotangent, token_owner),
        ],
        axis=1,
    )
    hidden_cotangent = (
        cotangent.astype(jnp.float32)
        + adapter_scale * expand_rows(second_cotangent, second_down_weight)
    ).astype(jnp.bfloat16)
    back_first = project(hidden_cotangent, first_up_weight).astype(jnp.bfloat16)
    grads_first = jnp.stack(
        [
            user_grads(back_first, activations, token_owner),
            user_grads(first_inner_state, hidden_cotangent, token_owner),
        ],
        axis=1,
    )
    shards_first, shards_second = (
        lax.psum_scatter(grads_first, "group", scatter_dimension=3, tiled=True),
        lax.psum_scatter(grads_second, "group", scatter_dimension=3, tiled=True),
    )
    local_squares = jnp.sum(shards_first * shards_first, axis=(1, 2, 3)) + jnp.sum(
        shards_second * shards_second, axis=(1, 2, 3)
    )
    squares = lax.psum(local_squares, "group")
    norms = jnp.sqrt(squares)
    clip_bound = (
        clip_norm_ratio[0]
        * adapter_scale
        * math.sqrt(4 * adapter_rank * model_width * user_sequences * sequence_length)
    )
    factor = clip_bound / jnp.maximum(norms, clip_bound)
    stacked = jnp.stack([shards_first, shards_second], axis=1)
    weighted = jnp.sum(factor[:, None, None, None, None] * stacked, axis=0)
    total_gradient = lax.psum(weighted, "dp")
    return total_gradient / (
        adapter_scale
        * math.sqrt(user_sequences * sequence_length * GROUP_USERS * lax.axis_size("dp"))
    )


def solution(mesh):
    return jax.shard_map(
        on_device,
        mesh=mesh,
        in_specs=(P(("dp", "group"), None), P(("dp", "group"), None), P(("dp", "group")), P(), P()),
        out_specs=P(None, None, None, "group"),
        check_vma=False,
    )
```

profile of v0, /device:TPU:1, one launch (start us, length us, event | category | flops | bytes accessed | tf_op | source)
XLA Modules:
  0.0 558.8 jit_solution(11417480318732018184)
XLA Ops:
  6.5 2.4 convolution_convert_fusion.1
  8.9 0.0 copy-start.5
  8.9 1.7 fusion.3
  10.7 0.0 copy-start.1
  10.7 0.6 convolution_convert_fusion
  11.3 1.7 copy-done.1
  13.0 0.6 convolution_convert_fusion.3
  13.7 0.7 fusion.2
  14.4 1.3 copy-done.4
  15.7 0.6 convolution_convert_fusion.2
  17.0 0.1 mul.106
  17.1 0.1 mul.107
  17.2 0.1 bitcast_multiply_fusion.3
  17.3 2.1 convolution_multiply_fusion.4
  19.3 0.5 convolution_multiply_fusion.5
  19.8 1.1 pad_maximum_fusion
  20.9 0.0 reduce-scatter.3.cloned.1.call-update
  20.9 0.0 reduce-scatter.5.cloned.1.call-start
  20.9 2.2 convolution_multiply_fusion.3
  23.1 0.5 convolution_multiply_fusion.2
  23.6 1.1 pad_maximum_fusion.1
  24.7 0.0 reduce-scatter.5.cloned.1.call-update
  24.7 0.0 all-reduce.2.cloned.1.call-start
  25.4 77.7 %reduce-scatter.3.cloned.1.call-done = f32[2,2,16,256]{3,2,0,1:T(8,128)} async-done(((f32[2,2,16,4096]{3,2,0,1:T(8,128)}), f32[2,2,16,256]{3,2,0,1:T(8,128)}) %reduce-scatter.3.cloned.1.call-update) | async-done | bytes 65552 | tf_op jit(solution)/shard_map/reduce_scatter | solution.py:79
  103.1 0.9 multiply_reduce_fusion.1
  104.1 87.1 %reduce-scatter.5.cloned.1.call-done = f32[2,2,16,256]{3,2,0,1:T(8,128)} async-done(((f32[2,2,16,4096]{3,2,0,1:T(8,128)}), f32[2,2,16,256]{3,2,0,1:T(8,128)}) %reduce-scatter.5.cloned.1.call-update) | async-done | bytes 65552 | tf_op jit(solution)/shard_map/reduce_scatter | solution.py:80
  191.2 0.9 multiply_reduce_fusion
  192.1 31.3 %psum.14 = f32[2]{0:T(128)S(1)} all-reduce(f32[2]{0:T(128)S(1)} %add.19), channel_id=1, replica_groups=mesh['dp'=32,'group'=16] {'group'}, use_global_device_ids=true, to_apply=%region_4.0 | all-reduce | flops 2 | bytes 16 | tf_op jit(solution)/shard_map/psum | solution.py:85
  223.5 1.6 fusion.4
  225.0 0.0 all-reduce.2.cloned.1.call-update
  225.1 325.7 %all-reduce.2.cloned.1.call-done = f32[2,2,16,256]{3,2,1,0:T(8,128)} async-done(((f32[2,2,16,256]{3,2,1,0:T(8,128)}), f32[2,2,16,256]{3,2,1,0:T(8,128)}) %all-reduce.2.cloned.1.call-update) | async-done | bytes 65552 | tf_op jit(solution)/shard_map/psum | solution.py:95
  550.8 1.5 broadcast_multiply_fusion
  (12 shorter events, 0.0 us)
Async XLA Ops:
  6.5 2.4 copy-start
  6.5 96.6 %reduce-scatter.3.cloned.1.call-start = ((), (), s32[]{:S(2)}) async-start(), calls=%async_computation.2 | async-start | bytes 1114112 | tf_op jit(solution)/shard_map/reduce_scatter | solution.py:79
  8.9 1.7 copy-start.5
  10.7 3.0 copy-start.3
  10.7 2.4 copy-start.1
  14.4 1.3 copy-start.4
  20.9 2.3 copy-start.2
  20.9 170.3 %reduce-scatter.5.cloned.1.call-start = ((), (), s32[]{:S(2)}) async-start(), calls=%async_computation.3 | async-start | bytes 1114112 | tf_op jit(solution)/shard_map/reduce_scatter | solution.py:80
  24.7 526.1 %all-reduce.2.cloned.1.call-start = ((), (), s32[]{:S(2)}) async-start(), calls=%async_computation.4 | async-start | bytes 131072 | tf_op jit(solution)/shard_map/psum | solution.py:95
Sparse Core Ops, SparseCore 0:
  21.0 82.0 reduce-scatter.2
  106.2 84.9 reduce-scatter.4
  225.2 325.5 all-reduce.1
where the time goes:
time: 559 us
  waiting for transfers between devices  491 us (88%)
  blocking collectives  31.3 us (6%)
  between operations  14.5 us (3%)
  matrix products  12 us (2%)
  other arithmetic  7.17 us (1%)
    psum x1, waiting for transfers between devices, on_device(): total_gradient = lax.psum(weighted, 'dp')  326 us
    reduce_scatter x1, waiting for transfers between devices, on_device(): lax.psum_scatter(grads_second, 'group', scatter_dimension=3, tiled=True)  87.1 us
    reduce_scatter x1, waiting for transfers between devices, on_device(): lax.psum_scatter(grads_first, 'group', scatter_dimension=3, tiled=True)  77.7 us
    psum x1, blocking collectives, on_device(): squares = lax.psum(local_squares, 'group')  31.3 us
  transfers between devices with their start and end apart: 3, of which 3 were waited for; matrix products, arithmetic and copies ran while one was open for 1% of the time, Pallas kernels for 0%

commit v1 on v0

v1 whole, which is shorter than its diff:
```python
import math

import jax
import jax.numpy as jnp
from jax import lax
from jax.experimental import pallas as pl
from jax.experimental.pallas import tpu as pltpu
from jax.sharding import Mesh, PartitionSpec as P

GROUP_USERS = 2
SCALE = 2.0
RANK = 16
WIDTH = 4096
TOKENS = 256
PEERS = 16
SLICE = WIDTH // PEERS
LANES = 128
ROWS = 4 * RANK * SLICE // LANES
SENT = ROWS + 8
USER_TOKENS = 8 * 256
N_DP = 32
CHUNK = 512

DP = ("z", "y_hi", "core")
GROUP = ("y_lo", "x")
VMEM = pl.BlockSpec(memory_space=pltpu.VMEM)
SMEM = pl.BlockSpec(memory_space=pltpu.SMEM)
F32 = jnp.float32
BF16 = jnp.bfloat16


def nt(a, b, precision=None):
    return lax.dot_general(
        a, b, (((1,), (1,)), ((), ())), preferred_element_type=F32, precision=precision
    )


def nn(a, b, precision=None):
    return jnp.dot(a, b, preferred_element_type=F32, precision=precision)


def gradient_kernel(x_ref, c_ref, adapters_ref, user_ref, out_ref):
    down1, up1 = adapters_ref[0, 0], adapters_ref[0, 1]
    down2, up2 = adapters_ref[1, 0], adapters_ref[1, 1]
    exact = lax.Precision.HIGHEST
    mixed = nt(down2, up1)
    from_x = nt(jnp.concatenate([down1, down2], axis=0), x_ref[...])
    from_c = nt(jnp.concatenate([up2, up1], axis=0), c_ref[...])
    z1 = from_x[:RANK].astype(BF16)
    q2 = from_c[:RANK].astype(BF16)
    z2 = (from_x[RANK:] + SCALE * nn(mixed, z1.astype(F32), exact)).astype(BF16)
    mixed_t = nt(up1, down2)
    q1 = (from_c[RANK:] + SCALE * nn(mixed_t, q2.astype(F32), exact)).astype(BF16)
    cross = (SCALE * SCALE) * nt(q2, z1)
    cross_t = (SCALE * SCALE) * nt(z1, q2)

    def split(value):
        high = value.astype(BF16)
        return jnp.concatenate([high, (value - high.astype(F32)).astype(BF16)], axis=0)

    cross2, cross2_t = split(cross), split(cross_t)
    left_x = jnp.concatenate([q1, q2], axis=0)
    left_c = jnp.concatenate([z1, z2], axis=0)
    for peer in range(PEERS):
        columns = pl.ds(peer * SLICE, SLICE)
        to_x = SCALE * nn(left_x, x_ref[:, columns])
        to_c = SCALE * nn(left_c, c_ref[:, columns])
        add_a2 = nn(cross2, adapters_ref[0, 1, :, columns])
        add_b1 = nn(cross2_t, adapters_ref[1, 0, :, columns])
        terms = (
            to_x[:RANK],
            to_c[:RANK] + (add_b1[:RANK] + add_b1[RANK:]),
            to_x[RANK:] + (add_a2[:RANK] + add_a2[RANK:]),
            to_c[RANK:],
        )
        for half in range(SLICE // LANES):
            for k, term in enumerate(terms):
                at = half * 4 * RANK + k * RANK
                out_ref[peer, at : at + RANK, :] = term[:, half * LANES : (half + 1) * LANES]
        out_ref[peer, ROWS:, :] = jnp.full((SENT - ROWS, LANES), user_ref[0].astype(F32), F32)


def users_kernel(got_ref, sums_ref, squares_ref):
    sums = [jnp.zeros((ROWS, LANES), F32) for _ in range(GROUP_USERS)]
    for peer in range(PEERS):
        term = got_ref[peer, :ROWS, :]
        owner = got_ref[peer, ROWS : ROWS + 1, :]
        for user in range(GROUP_USERS):
            sums[user] += jnp.where(owner == float(user), term, 0.0)
    for user in range(GROUP_USERS):
        sums_ref[user] = sums[user]
        total = jnp.sum(jnp.sum(sums[user] * sums[user], axis=0, keepdims=True), axis=1, keepdims=True)
        squares_ref[:, user, :] = jnp.broadcast_to(total, (PEERS, LANES))


def clip_kernel(ratio_ref, squares_ref, sums_ref, out_ref):
    bound = ratio_ref[0] * (SCALE * math.sqrt(4 * RANK * WIDTH * USER_TOKENS))
    squares = jnp.sum(squares_ref[...], axis=0)
    factor = bound / jnp.maximum(jnp.sqrt(squares), bound)
    total = factor[0:1] * sums_ref[0]
    for user in range(1, GROUP_USERS):
        total += factor[user : user + 1] * sums_ref[user]
    out_ref[...] = total


def on_device(activations, cotangent, user_ids, adapters, clip_norm_ratio):
    params = pltpu.CompilerParams(vmem_limit_bytes=40 * 1024 * 1024)
    terms = pl.pallas_call(
        gradient_kernel,
        out_shape=jax.ShapeDtypeStruct((PEERS, SENT, LANES), F32),
        in_specs=[VMEM, VMEM, VMEM, SMEM],
        out_specs=VMEM,
        compiler_params=params,
    )(activations, cotangent, adapters, user_ids)
    got = lax.all_to_all(terms, GROUP, 0, 0, tiled=True)
    sums, squares = pl.pallas_call(
        users_kernel,
        out_shape=(
            jax.ShapeDtypeStruct((GROUP_USERS, ROWS, LANES), F32),
            jax.ShapeDtypeStruct((PEERS, GROUP_USERS, LANES), F32),
        ),
        in_specs=[VMEM],
        out_specs=(VMEM, VMEM),
        compiler_params=params,
    )(got)
    squares = lax.all_to_all(squares, GROUP, 0, 0, tiled=True)
    total = pl.pallas_call(
        clip_kernel,
        out_shape=jax.ShapeDtypeStruct((ROWS, LANES), F32),
        in_specs=[SMEM, VMEM, VMEM],
        out_specs=VMEM,
        compiler_params=params,
    )(clip_norm_ratio, squares, sums)
    total += lax.ppermute(total, "core", [(0, 1), (1, 0)])
    total += lax.ppermute(total, "y_hi", [(0, 1), (1, 0)])
    ring = lax.axis_size("z")
    parts = lax.all_to_all(jnp.broadcast_to(total[None], (ring, ROWS, LANES)), "z", 0, 0, tiled=True)
    total = jnp.sum(parts, axis=0) / (SCALE * math.sqrt(USER_TOKENS * GROUP_USERS * N_DP))
    total = total.reshape(SLICE // LANES, 2, 2, RANK, LANES)
    return total.transpose(1, 2, 3, 0, 4).reshape(2, 2, RANK, SLICE)


def solution(mesh):
    fine = Mesh(mesh.devices.reshape(8, 2, 2, 4, 4), DP + GROUP)
    rows = P(DP + GROUP)
    return jax.shard_map(
        on_device,
        mesh=fine,
        in_specs=(rows, rows, rows, P(), P()),
        out_specs=P(None, None, None, GROUP),
        check_vma=False,
    )
```

time: 559 us -> 98.5 us (0.18)
  the two profiles are of different devices: /device:TPU:1 before, /device:TPU:8 now
where the time goes in v1:
time: 98.5 us; the launch traced here: 98.1 us
  blocking collectives  63 us (64%)
  waiting for transfers between devices  13.5 us (14%)
  starting transfers between devices  11.9 us (12%)
  local copies, waits for them, and re-layouts  4.89 us (5%)
  Pallas kernels  3.29 us (3%)
  between operations  1.37 us (1%)
    all_to_all x1, blocking collectives, on_device(): got = lax.all_to_all(terms, GROUP, 0, 0, tiled=True)  35.5 us
    all_to_all x1, blocking collectives, on_device(): lax.all_to_all(jnp.broadcast_to(total[None], (ring, ROWS, LANES)), 'z', 0...  27.6 us
    ppermute x1, waiting for transfers between devices, on_device(): total += lax.ppermute(total, 'y_hi', [(0, 1), (1, 0)])  6.44 us
    all_to_all x1, waiting for transfers between devices, on_device(): squares = lax.all_to_all(squares, GROUP, 0, 0, tiled=True)  5.88 us
    all_to_all x1, starting transfers between devices, on_device(): squares = lax.all_to_all(squares, GROUP, 0, 0, tiled=True)  5.08 us
    ppermute x1, starting transfers between devices, on_device(): total += lax.ppermute(total, 'y_hi', [(0, 1), (1, 0)])  4.91 us
    unnamed x6, local copies, waits for them, and re-layouts  4.22 us
    pallas_call x1, Pallas kernels, on_device(): pl.pallas_call(gradient_kernel, out_shape=jax.ShapeDtypeStruct((PEERS, SE...  2.39 us
  transfers between devices with their start and end apart: 3, of which 3 were waited for; matrix products, arithmetic and copies ran while one was open for 0% of the time, Pallas kernels for 0%

profile of v1, /device:TPU:8, one launch (start us, length us, event | category | flops | bytes accessed | tf_op | source)
XLA Modules:
  0.0 98.1 jit_solution(7240109715071561988)
XLA Ops:
  0.7 0.0 copy-start
  0.7 1.6 %copy-done = bf16[256,4096]{1,0:T(8,128)(2,1)S(1)} copy-done((bf16[256,4096]{1,0:T(8,128)(2,1)S(1)}, bf16[256,4096]{1,0:T(8,128)(2,1)}, u32[]{:S(2)}) %copy-start) | copy-done | bytes 2097176
  2.2 0.0 copy-start.1
  2.2 1.6 %copy-done.1 = bf16[256,4096]{1,0:T(8,128)(2,1)S(1)} copy-done((bf16[256,4096]{1,0:T(8,128)(2,1)S(1)}, bf16[256,4096]{1,0:T(8,128)(2,1)}, u32[]{:S(2)}) %copy-start.1) | copy-done | bytes 2097176
  3.8 0.0 copy-start.2
  3.8 1.0 %copy-done.2 = bf16[2,2,16,4096]{3,2,1,0:T(8,128)(2,1)S(1)} copy-done((bf16[2,2,16,4096]{3,2,1,0:T(8,128)(2,1)S(1)}, bf16[2,2,16,4096]{3,2,1,0:T(8,128)(2,1)}, u32[]{:S(2)}) %copy-start.2) | copy-done | bytes 524312
  4.9 2.4 %shard_map.55 = f32[16,136,128]{2,1,0:T(8,128)S(1)} custom-call(bf16[256,4096]{1,0:T(8,128)(2,1)S(1)} %copy-done, bf16[256,4096]{1,0:T(8,128)(2,1)S(1)} %copy-done.1, bf16[2,2,16,4096]{3,2,1,0:T(8,128)(2,1)S(1)} %copy-done.2, s32[1]{0:T(128)S(6)} %copy.11.user_ref), custom_call_target="tpu_custom_call" | custom-call | tf_op jit(solution)/shard_map/pallas_call | solution.py:108
  7.3 35.5 %all_to_all.15.got_ref = f32[16,136,128]{2,1,0:T(8,128)S(1)} all-to-all(f32[16,136,128]{2,1,0:T(8,128)S(1)} %shard_map.55), channel_id=1, replica_groups=mesh['z'=8,'y_hi'=2,'core'=2,'y_lo'=4,'x'=4] {'y_lo','x'}, dimensions={0} | all-to-all | bytes 2228224 | tf_op jit(solution)/shard_map/all_to_all | solution.py:115
  42.7 0.9 shard_map.56
  43.6 5.1 %all-to-all-start.1 = ((f32[16,2,128]{2,1,0:T(2,128)}), f32[16,2,128]{2,1,0:T(2,128)S(1)}, u32[]{:S(2)}, u32[]{:S(2)}) async-start(f32[16,2,128]{2,1,0:T(2,128)} %get-tuple-element.7), calls=%async_computation.1 | async-start | bytes 32768 | tf_op jit(solution)/shard_map/all_to_all | solution.py:126
  49.3 5.9 %all-to-all-done.1.squares_ref = f32[16,2,128]{2,1,0:T(2,128)S(1)} async-done(((f32[16,2,128]{2,1,0:T(2,128)}), f32[16,2,128]{2,1,0:T(2,128)S(1)}, u32[]{:S(2)}, u32[]{:S(2)}) %all-to-all-start.1) | async-done | bytes 16416 | tf_op jit(solution)/shard_map/all_to_all | solution.py:126
  55.3 1.9 %collective-permute-start = (f32[128,128]{1,0:T(8,128)S(1)}, f32[128,128]{1,0:T(8,128)S(1)}, u32[]{:S(2)}, u32[]{:S(2)}) collective-permute-start(f32[128,128]{1,0:T(8,128)S(1)} %shard_map.57), channel_id=1, source_target_pairs={{0,16},{16,0},{1,17},{17,1},{2,18},{18,2},{3,19},{19,3},{4,20},{20... | collective-permute-start | bytes 196616 | tf_op jit(solution)/shard_map/ppermute | solution.py:134
  57.2 1.2 %collective-permute-done = f32[128,128]{1,0:T(8,128)S(1)} collective-permute-done((f32[128,128]{1,0:T(8,128)S(1)}, f32[128,128]{1,0:T(8,128)S(1)}, u32[]{:S(2)}, u32[]{:S(2)}) %collective-permute-start) | collective-permute-done | bytes 65568 | tf_op jit(solution)/shard_map/ppermute | solution.py:134
  58.4 4.9 %collective-permute-start.1 = (f32[128,128]{1,0:T(8,128)S(1)}, f32[128,128]{1,0:T(8,128)S(1)}, u32[]{:S(2)}, u32[]{:S(2)}) collective-permute-start(f32[128,128]{1,0:T(8,128)S(1)} %add.6), channel_id=1, source_target_pairs={{0,32},{32,0},{1,33},{33,1},{2,34},{34,2},{3,35},{35,3},{4,36},{36... | collective-permute-start | bytes 196616 | tf_op jit(solution)/shard_map/ppermute | solution.py:135
  63.3 6.4 %collective-permute-done.1 = f32[128,128]{1,0:T(8,128)S(1)} collective-permute-done((f32[128,128]{1,0:T(8,128)S(1)}, f32[128,128]{1,0:T(8,128)S(1)}, u32[]{:S(2)}, u32[]{:S(2)}) %collective-permute-start.1) | collective-permute-done | bytes 65568 | tf_op jit(solution)/shard_map/ppermute | solution.py:135
  69.8 27.6 %all_to_all.16 = f32[8,128,128]{2,1,0:T(8,128)S(1)} all-to-all(f32[8,128,128]{2,1,0:T(8,128)S(1)} %broadcast_in_dim.2), channel_id=1, replica_groups=mesh['z'=8,'y_hi'=2,'core'=2,'y_lo'=4,'x'=4] {'z'}, dimensions={0} | all-to-all | bytes 1048576 | tf_op jit(solution)/shard_map/all_to_all | solution.py:137
  97.5 0.6 copy.10
  (6 shorter events, 0.1 us)
Async XLA Ops:
  0.7 1.6 %copy-start = (bf16[256,4096]{1,0:T(8,128)(2,1)S(1)}, bf16[256,4096]{1,0:T(8,128)(2,1)}, u32[]{:S(2)}) copy-start(bf16[256,4096]{1,0:T(8,128)(2,1)} %x_ref.1) | copy-start | bytes 6291460
  2.2 1.6 %copy-start.1 = (bf16[256,4096]{1,0:T(8,128)(2,1)S(1)}, bf16[256,4096]{1,0:T(8,128)(2,1)}, u32[]{:S(2)}) copy-start(bf16[256,4096]{1,0:T(8,128)(2,1)} %c_ref.1) | copy-start | bytes 6291460
  3.8 1.0 %copy-start.2 = (bf16[2,2,16,4096]{3,2,1,0:T(8,128)(2,1)S(1)}, bf16[2,2,16,4096]{3,2,1,0:T(8,128)(2,1)}, u32[]{:S(2)}) copy-start(bf16[2,2,16,4096]{3,2,1,0:T(8,128)(2,1)} %adapters_ref.1) | copy-start | bytes 1572868
  43.6 11.6 %all-to-all-start.1 = ((f32[16,2,128]{2,1,0:T(2,128)}), f32[16,2,128]{2,1,0:T(2,128)S(1)}, u32[]{:S(2)}, u32[]{:S(2)}) async-start(f32[16,2,128]{2,1,0:T(2,128)} %get-tuple-element.7), calls=%async_computation.1 | async-start | bytes 32768 | tf_op jit(solution)/shard_map/all_to_all | solution.py:126
  55.3 3.1 %collective-permute-start = (f32[128,128]{1,0:T(8,128)S(1)}, f32[128,128]{1,0:T(8,128)S(1)}, u32[]{:S(2)}, u32[]{:S(2)}) collective-permute-start(f32[128,128]{1,0:T(8,128)S(1)} %shard_map.57), channel_id=1, source_target_pairs={{0,16},{16,0},{1,17},{17,1},{2,18},{18,2},{3,19},{19,3},{4,20},{20... | collective-permute-start | bytes 196616 | tf_op jit(solution)/shard_map/ppermute | solution.py:134
  58.4 11.4 %collective-permute-start.1 = (f32[128,128]{1,0:T(8,128)S(1)}, f32[128,128]{1,0:T(8,128)S(1)}, u32[]{:S(2)}, u32[]{:S(2)}) collective-permute-start(f32[128,128]{1,0:T(8,128)S(1)} %add.6), channel_id=1, source_target_pairs={{0,32},{32,0},{1,33},{33,1},{2,34},{34,2},{3,35},{35,3},{4,36},{36... | collective-permute-start | bytes 196616 | tf_op jit(solution)/shard_map/ppermute | solution.py:135

commit v2 on v1

v2 whole, which is shorter than its diff:
```python
import math

import jax
import jax.numpy as jnp
from jax import lax
from jax.experimental import pallas as pl
from jax.experimental.pallas import tpu as pltpu
from jax.sharding import Mesh, PartitionSpec as P

GROUP_USERS = 2
SCALE = 2.0
RANK = 16
WIDTH = 4096
TOKENS = 256
PEERS = 16
SLICE = WIDTH // PEERS
LANES = 128
HALF = 4 * RANK
ROWS = HALF * SLICE // LANES
SENT = ROWS + 8
USER_TOKENS = 8 * 256
N_DP = 32
PARTS = 4
PART = WIDTH // PARTS
RING = 8

DP = ("z", "y_hi", "core")
GROUP = ("y_lo", "x")
VMEM = pl.BlockSpec(memory_space=pltpu.VMEM)
SMEM = pl.BlockSpec(memory_space=pltpu.SMEM)
HBM = pl.BlockSpec(memory_space=pltpu.HBM)
F32 = jnp.float32
BF16 = jnp.bfloat16
PARAMS = pltpu.CompilerParams(vmem_limit_bytes=40 * 1024 * 1024)
WIDE = pltpu.CompilerParams(vmem_limit_bytes=60 * 1024 * 1024)


def shape(*dims):
    return jax.ShapeDtypeStruct(dims, F32)


def nt(a, b, precision=None):
    return lax.dot_general(
        a, b, (((1,), (1,)), ((), ())), preferred_element_type=F32, precision=precision
    )


def nn(a, b, precision=None):
    return jnp.dot(a, b, preferred_element_type=F32, precision=precision)


def split(value):
    high = value.astype(BF16)
    return jnp.concatenate([high, (value - high.astype(F32)).astype(BF16)], axis=0)


def halves(value):
    return value[:RANK] + value[RANK:]


def gradient_kernel(
    x_hbm, c_hbm, adapters_hbm, user_ref, out_hbm, x_ref, c_ref, adapters_ref, out_ref, sems, out_sems
):
    copies = []
    for part in range(PARTS):
        at = pl.ds(part * PART, PART)
        copies.append(
            (
                pltpu.make_async_copy(adapters_hbm.at[:, :, :, at], adapters_ref.at[:, :, :, at], sems.at[0, part]),
                pltpu.make_async_copy(x_hbm.at[:, at], x_ref.at[:, at], sems.at[1, part]),
                pltpu.make_async_copy(c_hbm.at[:, at], c_ref.at[:, at], sems.at[2, part]),
            )
        )
    for group in copies:
        for copy in group:
            copy.start()
    from_x = jnp.zeros((2 * RANK, TOKENS), F32)
    from_c = jnp.zeros((2 * RANK, TOKENS), F32)
    mixed = jnp.zeros((RANK, RANK), F32)
    mixed_t = jnp.zeros((RANK, RANK), F32)
    for part in range(PARTS):
        for copy in copies[part]:
            copy.wait()
        at = pl.ds(part * PART, PART)
        down1, up1 = adapters_ref[0, 0, :, at], adapters_ref[0, 1, :, at]
        down2, up2 = adapters_ref[1, 0, :, at], adapters_ref[1, 1, :, at]
        from_x += nt(jnp.concatenate([down1, down2], axis=0), x_ref[:, at])
        from_c += nt(jnp.concatenate([up2, up1], axis=0), c_ref[:, at])
        mixed += nt(down2, up1)
        mixed_t += nt(up1, down2)
    exact = lax.Precision.HIGHEST
    z1 = from_x[:RANK].astype(BF16)
    q2 = from_c[:RANK].astype(BF16)
    z2 = (from_x[RANK:] + SCALE * nn(mixed, z1.astype(F32), exact)).astype(BF16)
    q1 = (from_c[RANK:] + SCALE * nn(mixed_t, q2.astype(F32), exact)).astype(BF16)
    cross = split((SCALE * SCALE) * nt(q2, z1))
    cross_t = split((SCALE * SCALE) * nt(z1, q2))
    left_x = jnp.concatenate([q1, q2], axis=0)
    left_c = jnp.concatenate([z1, z2], axis=0)
    sends = []
    for peer in range(PEERS):
        columns = pl.ds(peer * SLICE, SLICE)
        to_x = SCALE * nn(left_x, x_ref[:, columns])
        to_c = SCALE * nn(left_c, c_ref[:, columns])
        add_a2 = halves(nn(cross, adapters_ref[0, 1, :, columns]))
        add_b1 = halves(nn(cross_t, adapters_ref[1, 0, :, columns]))
        terms = (to_x[:RANK], to_c[:RANK] + add_b1, to_x[RANK:] + add_a2, to_c[RANK:])
        for half in range(SLICE // LANES):
            for k, term in enumerate(terms):
                at = half * HALF + k * RANK
                out_ref[peer, at : at + RANK, :] = term[:, half * LANES : (half + 1) * LANES]
        out_ref[peer, ROWS:, :] = jnp.full((SENT - ROWS, LANES), user_ref[0].astype(F32), F32)
        send = pltpu.make_async_copy(out_ref.at[peer], out_hbm.at[peer], out_sems.at[peer])
        send.start()
        sends.append(send)
    for send in sends:
        send.wait()


def users_kernel(got_ref, sums_ref, squares_ref):
    sums = [jnp.zeros((ROWS, LANES), F32) for _ in range(GROUP_USERS)]
    for peer in range(PEERS):
        term = got_ref[peer, :ROWS, :]
        owner = got_ref[peer, ROWS : ROWS + 1, :]
        for user in range(GROUP_USERS):
            sums[user] += jnp.where(owner == float(user), term, 0.0)
    for user in range(GROUP_USERS):
        sums_ref[user] = sums[user]
        square = jnp.sum(jnp.sum(sums[user] * sums[user], axis=0, keepdims=True), axis=1, keepdims=True)
        squares_ref[:, user, :] = jnp.broadcast_to(square, (PEERS, LANES))


def clip_kernel(ratio_ref, squares_ref, sums_ref, out_ref):
    bound = ratio_ref[0] * (SCALE * math.sqrt(4 * RANK * WIDTH * USER_TOKENS))
    squares = jnp.sum(squares_ref[...], axis=0)
    factor = bound / jnp.maximum(jnp.sqrt(squares), bound)
    total = factor[0:1] * sums_ref[0]
    for user in range(1, GROUP_USERS):
        total += factor[user : user + 1] * sums_ref[user]
    for half in range(SLICE // LANES):
        out_ref[half] = total[half * HALF : (half + 1) * HALF]


def chip_kernel(core_ref, pair_ref, out_ref):
    core = core_ref[0]
    out_ref[...] = pair_ref[0, core] + pair_ref[1, core]


def spread_kernel(pair_ref, out_ref):
    out_ref[...] = jnp.broadcast_to((pair_ref[0] + pair_ref[1])[None], (RING, HALF, LANES))


def total_kernel(parts_ref, out_ref):
    total = parts_ref[0]
    for part in range(1, RING):
        total += parts_ref[part]
    out_ref[...] = total / (SCALE * math.sqrt(USER_TOKENS * GROUP_USERS * N_DP))


def call(kernel, out_shape, *args, scalars=0):
    several = isinstance(out_shape, tuple)
    return pl.pallas_call(
        kernel,
        out_shape=out_shape,
        in_specs=[SMEM] * scalars + [VMEM] * (len(args) - scalars),
        out_specs=(VMEM,) * len(out_shape) if several else VMEM,
        compiler_params=PARAMS,
    )(*args)


def on_device(activations, cotangent, user_ids, adapters, clip_norm_ratio):
    terms = pl.pallas_call(
        gradient_kernel,
        out_shape=shape(PEERS, SENT, LANES),
        in_specs=[HBM, HBM, HBM, SMEM],
        out_specs=HBM,
        scratch_shapes=[
            pltpu.VMEM((TOKENS, WIDTH), BF16),
            pltpu.VMEM((TOKENS, WIDTH), BF16),
            pltpu.VMEM((2, 2, RANK, WIDTH), BF16),
            pltpu.VMEM((PEERS, SENT, LANES), F32),
            pltpu.SemaphoreType.DMA((3, PARTS)),
            pltpu.SemaphoreType.DMA((PEERS,)),
        ],
        compiler_params=WIDE,
    )(activations, cotangent, adapters, user_ids)
    terms = lax.all_to_all(terms, GROUP, 0, 0, tiled=True)
    sums, squares = call(
        users_kernel, (shape(GROUP_USERS, ROWS, LANES), shape(PEERS, GROUP_USERS, LANES)), terms
    )
    squares = lax.all_to_all(squares, GROUP, 0, 0, tiled=True)
    clipped = call(clip_kernel, shape(2, HALF, LANES), clip_norm_ratio, squares, sums, scalars=1)
    pair = lax.all_gather(clipped, "core")
    core = lax.axis_index("core")[None]
    chip = call(chip_kernel, shape(HALF, LANES), core, pair, scalars=1)
    parts = call(spread_kernel, shape(RING, HALF, LANES), lax.all_gather(chip, "y_hi"))
    parts = lax.all_to_all(parts, "z", 0, 0, tiled=True)
    total = call(total_kernel, shape(HALF, LANES), parts)
    total = lax.all_gather(total, "core", axis=1, tiled=True)
    return total.reshape(2, 2, RANK, SLICE)


def solution(mesh):
    fine = Mesh(mesh.devices.reshape(8, 2, 2, 4, 4), DP + GROUP)
    rows = P(DP + GROUP)
    return jax.shard_map(
        on_device,
        mesh=fine,
        in_specs=(rows, rows, rows, P(), P()),
        out_specs=P(None, None, None, GROUP),
        check_vma=False,
    )
```

time: 98.5 us -> 90.5 us (0.919)
  the two profiles are of different devices: /device:TPU:8 before, /device:TPU:1 now
where the time goes in v2:
time: 90.5 us; the launch traced here: 90.2 us
  blocking collectives  71.5 us (79%)
  waiting for transfers between devices  6.2 us (7%)
  Pallas kernels  6.01 us (7%)
  starting transfers between devices  4.52 us (5%)
  between operations  1.34 us (1%)
    all_to_all x1, blocking collectives, on_device(): terms = lax.all_to_all(terms, GROUP, 0, 0, tiled=True)  35.4 us
    all_to_all x1, blocking collectives, on_device(): parts = lax.all_to_all(parts, 'z', 0, 0, tiled=True)  19 us
    all_gather x1, blocking collectives, on_device(): lax.all_gather(chip, 'y_hi')  7.34 us
    all_to_all x1, waiting for transfers between devices, on_device(): squares = lax.all_to_all(squares, GROUP, 0, 0, tiled=True)  6.2 us
    all_gather x1, blocking collectives, on_device(): total = lax.all_gather(total, 'core', axis=1, tiled=True)  5.15 us
    pallas_call x1, Pallas kernels, on_device(): pl.pallas_call(gradient_kernel, out_shape=shape(PEERS, SENT, LANES), in_s...  5.07 us
    all_gather x1, blocking collectives, on_device(): pair = lax.all_gather(clipped, 'core')  4.63 us
    all_to_all x1, starting transfers between devices, on_device(): squares = lax.all_to_all(squares, GROUP, 0, 0, tiled=True)  4.52 us
  transfers between devices with their start and end apart: 1, of which 1 were waited for; matrix products, arithmetic and copies ran while one was open for 0% of the time, Pallas kernels for 0%

profile of v2, /device:TPU:1, one launch (start us, length us, event | category | flops | bytes accessed | tf_op | source)
XLA Modules:
  0.0 90.2 jit_solution(2946069377621325013)
XLA Ops:
  0.7 5.1 %shard_map.55 = f32[16,136,128]{2,1,0:T(8,128)} custom-call(bf16[256,4096]{1,0:T(8,128)(2,1)} %x_hbm.1, bf16[256,4096]{1,0:T(8,128)(2,1)} %c_hbm.1, bf16[2,2,16,4096]{3,2,1,0:T(8,128)(2,1)} %adapters_hbm.1, s32[1]{0:T(128)S(6)} %copy.7.user_ref), custom_call_target="tpu_custom_call" | custom-call | tf_op jit(solution)/shard_map/pallas_call | solution.py:172
  5.7 35.4 %all_to_all.15.got_ref = f32[16,136,128]{2,1,0:T(8,128)S(1)} all-to-all(f32[16,136,128]{2,1,0:T(8,128)} %shard_map.55), channel_id=1, replica_groups=mesh['z'=8,'y_hi'=2,'core'=2,'y_lo'=4,'x'=4] {'y_lo','x'}, dimensions={0} | all-to-all | bytes 2228224 | tf_op jit(solution)/shard_map/all_to_all | solution.py:187
  41.1 0.9 shard_map.56
  42.0 4.5 %all-to-all-start.1 = ((f32[16,2,128]{2,1,0:T(2,128)}), f32[16,2,128]{2,1,0:T(2,128)S(1)}, u32[]{:S(2)}, u32[]{:S(2)}) async-start(f32[16,2,128]{2,1,0:T(2,128)} %get-tuple-element.7), calls=%async_computation.1 | async-start | bytes 32768 | tf_op jit(solution)/shard_map/all_to_all | solution.py:191
  47.1 6.2 %all-to-all-done.1.squares_ref = f32[16,2,128]{2,1,0:T(2,128)S(1)} async-done(((f32[16,2,128]{2,1,0:T(2,128)}), f32[16,2,128]{2,1,0:T(2,128)S(1)}, u32[]{:S(2)}, u32[]{:S(2)}) %all-to-all-start.1) | async-done | bytes 16416 | tf_op jit(solution)/shard_map/all_to_all | solution.py:191
  53.4 4.6 %all-gather = f32[4,64,128]{2,1,0:T(8,128)S(1)} all-gather(f32[2,64,128]{2,1,0:T(8,128)S(1)} %shard_map.57), channel_id=2, replica_groups=mesh['z'=8,'y_hi'=2,'core'=2,'y_lo'=4,'x'=4] {'core'}, dimensions={0}, use_global_device_ids=true | all-gather | bytes 196608 | tf_op jit(solution)/shard_map/all_gather | solution.py:193
  58.0 7.3 %all-gather.1 = f32[128,128]{1,0:T(8,128)S(1)} all-gather(f32[64,128]{1,0:T(8,128)S(1)} %shard_map.58), channel_id=3, replica_groups=mesh['z'=8,'y_hi'=2,'core'=2,'y_lo'=4,'x'=4] {'y_hi'}, dimensions={0}, use_global_device_ids=true | all-gather | bytes 98304 | tf_op jit(solution)/shard_map/all_gather | solution.py:196
  65.4 19.0 %all_to_all.16.parts_ref = f32[8,64,128]{2,1,0:T(8,128)S(1)} all-to-all(f32[8,64,128]{2,1,0:T(8,128)S(1)} %shard_map.59), channel_id=1, replica_groups=mesh['z'=8,'y_hi'=2,'core'=2,'y_lo'=4,'x'=4] {'z'}, dimensions={0} | all-to-all | bytes 524288 | tf_op jit(solution)/shard_map/all_to_all | solution.py:197
  84.4 5.1 %all_gather.19 = f32[64,256]{1,0:T(8,128)S(1)} all-gather(f32[64,128]{1,0:T(8,128)S(1)} %shard_map.60), channel_id=1, replica_groups=mesh['z'=8,'y_hi'=2,'core'=2,'y_lo'=4,'x'=4] {'core'}, dimensions={1}, use_global_device_ids=true | all-gather | bytes 98304 | tf_op jit(solution)/shard_map/all_gather | solution.py:199
  89.6 0.6 copy.9
  (4 shorter events, 0.1 us)
Async XLA Ops:
  42.0 11.4 %all-to-all-start.1 = ((f32[16,2,128]{2,1,0:T(2,128)}), f32[16,2,128]{2,1,0:T(2,128)S(1)}, u32[]{:S(2)}, u32[]{:S(2)}) async-start(f32[16,2,128]{2,1,0:T(2,128)} %get-tuple-element.7), calls=%async_computation.1 | async-start | bytes 32768 | tf_op jit(solution)/shard_map/all_to_all | solution.py:191

commit v3 on v2

--- a/solution.py
+++ b/solution.py
@@ -12,12 +12,15 @@
 RANK = 16
 WIDTH = 4096
 TOKENS = 256
-PEERS = 16
+NEAR = 8
+FAR = 2
+PEERS = NEAR * FAR
+CORES = 2
 SLICE = WIDTH // PEERS
 LANES = 128
 HALF = 4 * RANK
 ROWS = HALF * SLICE // LANES
-SENT = ROWS + 8
+SENT = FAR * ROWS + 8
 USER_TOKENS = 8 * 256
 N_DP = 32
 PARTS = 4
@@ -25,7 +28,7 @@
 RING = 8
 
 DP = ("z", "y_hi", "core")
-GROUP = ("y_lo", "x")
+GROUP = ("y_mid", "y_low", "x")
 VMEM = pl.BlockSpec(memory_space=pltpu.VMEM)
 SMEM = pl.BlockSpec(memory_space=pltpu.SMEM)
 HBM = pl.BlockSpec(memory_space=pltpu.HBM)
@@ -98,52 +101,59 @@
     left_x = jnp.concatenate([q1, q2], axis=0)
     left_c = jnp.concatenate([z1, z2], axis=0)
     sends = []
-    for peer in range(PEERS):
-        columns = pl.ds(peer * SLICE, SLICE)
-        to_x = SCALE * nn(left_x, x_ref[:, columns])
-        to_c = SCALE * nn(left_c, c_ref[:, columns])
-        add_a2 = halves(nn(cross, adapters_ref[0, 1, :, columns]))
-        add_b1 = halves(nn(cross_t, adapters_ref[1, 0, :, columns]))
-        terms = (to_x[:RANK], to_c[:RANK] + add_b1, to_x[RANK:] + add_a2, to_c[RANK:])
-        for half in range(SLICE // LANES):
-            for k, term in enumerate(terms):
-                at = half * HALF + k * RANK
-                out_ref[peer, at : at + RANK, :] = term[:, half * LANES : (half + 1) * LANES]
-        out_ref[peer, ROWS:, :] = jnp.full((SENT - ROWS, LANES), user_ref[0].astype(F32), F32)
-        send = pltpu.make_async_copy(out_ref.at[peer], out_hbm.at[peer], out_sems.at[peer])
+    for near in range(NEAR):
+        for far in range(FAR):
+            columns = pl.ds((far * NEAR + near) * SLICE, SLICE)
+            to_x = SCALE * nn(left_x, x_ref[:, columns])
+            to_c = SCALE * nn(left_c, c_ref[:, columns])
+            add_a2 = halves(nn(cross, adapters_ref[0, 1, :, columns]))
+            add_b1 = halves(nn(cross_t, adapters_ref[1, 0, :, columns]))
+            terms = (to_x[:RANK], to_c[:RANK] + add_b1, to_x[RANK:] + add_a2, to_c[RANK:])
+            for half in range(SLICE // LANES):
+                for k, term in enumerate(terms):
+                    at = far * ROWS + half * HALF + k * RANK
+                    out_ref[near, at : at + RANK, :] = term[:, half * LANES : (half + 1) * LANES]
+        out_ref[near, FAR * ROWS :, :] = jnp.full((SENT - FAR * ROWS, LANES), user_ref[0].astype(F32), F32)
+        send = pltpu.make_async_copy(out_ref.at[near], out_hbm.at[near], out_sems.at[near])
         send.start()
         sends.append(send)
     for send in sends:
         send.wait()
 
 
-def users_kernel(got_ref, sums_ref, squares_ref):
-    sums = [jnp.zeros((ROWS, LANES), F32) for _ in range(GROUP_USERS)]
-    for peer in range(PEERS):
-        term = got_ref[peer, :ROWS, :]
-        owner = got_ref[peer, ROWS : ROWS + 1, :]
+def users_kernel(mid_ref, got_ref, keep_ref, send_ref):
+    mid = mid_ref[0]
+    for far, out_ref in ((mid, keep_ref), (1 - mid, send_ref)):
+        rows = pl.ds(pl.multiple_of(far * ROWS, ROWS), ROWS)
+        sums = [jnp.zeros((ROWS, LANES), F32) for _ in range(GROUP_USERS)]
+        for near in range(NEAR):
+            term = got_ref[near, rows, :]
+            owner = got_ref[near, FAR * ROWS : FAR * ROWS + 1, :]
+            for user in range(GROUP_USERS):
+                sums[user] += jnp.where(owner == float(user), term, 0.0)
         for user in range(GROUP_USERS):
-            sums[user] += jnp.where(owner == float(user), term, 0.0)
+            out_ref[user] = sums[user]
+
+
+def squares_kernel(mid_ref, keep_ref, got_ref, sums_ref, squares_ref):
+    partner = 1 - mid_ref[0]
     for user in range(GROUP_USERS):
-        sums_ref[user] = sums[user]
-        square = jnp.sum(jnp.sum(sums[user] * sums[user], axis=0, keepdims=True), axis=1, keepdims=True)
-        squares_ref[:, user, :] = jnp.broadcast_to(square, (PEERS, LANES))
-
-
-def clip_kernel(ratio_ref, squares_ref, sums_ref, out_ref):
+        total = keep_ref[user] + got_ref[partner, user]
+        sums_ref[user] = total
+        square = jnp.sum(jnp.sum(total * total, axis=0, keepdims=True), axis=1, keepdims=True)
+        squares_ref[:, user, :] = jnp.broadcast_to(square, (CORES * PEERS, LANES))
+
+
+def clip_kernel(core_ref, ratio_ref, squares_ref, sums_ref, out_ref):
+    rows = pl.ds(pl.multiple_of(core_ref[0] * HALF, HALF), HALF)
     bound = ratio_ref[0] * (SCALE * math.sqrt(4 * RANK * WIDTH * USER_TOKENS))
-    squares = jnp.sum(squares_ref[...], axis=0)
-    factor = bound / jnp.maximum(jnp.sqrt(squares), bound)
-    total = factor[0:1] * sums_ref[0]
-    for user in range(1, GROUP_USERS):
-        total += factor[user : user + 1] * sums_ref[user]
-    for half in range(SLICE // LANES):
-        out_ref[half] = total[half * HALF : (half + 1) * HALF]
-
-
-def chip_kernel(core_ref, pair_ref, out_ref):
-    core = core_ref[0]
-    out_ref[...] = pair_ref[0, core] + pair_ref[1, core]
+    total = jnp.zeros((HALF, LANES), F32)
+    for core in range(CORES):
+        squares = jnp.sum(squares_ref[core * PEERS : (core + 1) * PEERS], axis=0)
+        factor = bound / jnp.maximum(jnp.sqrt(squares), bound)
+        for user in range(GROUP_USERS):
+            total += factor[user : user + 1] * sums_ref[core, user, rows, :]
+    out_ref[...] = total
 
 
 def spread_kernel(pair_ref, out_ref):
@@ -169,30 +179,32 @@
 
 
 def on_device(activations, cotangent, user_ids, adapters, clip_norm_ratio):
+    mid, core = lax.axis_index("y_mid")[None], lax.axis_index("core")[None]
     terms = pl.pallas_call(
         gradient_kernel,
-        out_shape=shape(PEERS, SENT, LANES),
+        out_shape=shape(NEAR, SENT, LANES),
         in_specs=[HBM, HBM, HBM, SMEM],
         out_specs=HBM,
         scratch_shapes=[
             pltpu.VMEM((TOKENS, WIDTH), BF16),
             pltpu.VMEM((TOKENS, WIDTH), BF16),
             pltpu.VMEM((2, 2, RANK, WIDTH), BF16),
-            pltpu.VMEM((PEERS, SENT, LANES), F32),
+            pltpu.VMEM((NEAR, SENT, LANES), F32),
             pltpu.SemaphoreType.DMA((3, PARTS)),
-            pltpu.SemaphoreType.DMA((PEERS,)),
+            pltpu.SemaphoreType.DMA((NEAR,)),
         ],
         compiler_params=WIDE,
     )(activations, cotangent, adapters, user_ids)
-    terms = lax.all_to_all(terms, GROUP, 0, 0, tiled=True)
+    terms = lax.all_to_all(terms, ("y_low", "x"), 0, 0, tiled=True)
+    users = shape(GROUP_USERS, ROWS, LANES)
+    keep, send = call(users_kernel, (users, users), mid, terms, scalars=1)
+    got = lax.all_gather(send, "y_mid")
     sums, squares = call(
-        users_kernel, (shape(GROUP_USERS, ROWS, LANES), shape(PEERS, GROUP_USERS, LANES)), terms
+        squares_kernel, (users, shape(CORES * PEERS, GROUP_USERS, LANES)), mid, keep, got, scalars=1
     )
-    squares = lax.all_to_all(squares, GROUP, 0, 0, tiled=True)
-    clipped = call(clip_kernel, shape(2, HALF, LANES), clip_norm_ratio, squares, sums, scalars=1)
-    pair = lax.all_gather(clipped, "core")
-    core = lax.axis_index("core")[None]
-    chip = call(chip_kernel, shape(HALF, LANES), core, pair, scalars=1)
+    squares = lax.all_to_all(squares, ("core",) + GROUP, 0, 0, tiled=True)
+    sums = lax.all_gather(sums, "core")
+    chip = call(clip_kernel, shape(HALF, LANES), core, clip_norm_ratio, squares, sums, scalars=2)
     parts = call(spread_kernel, shape(RING, HALF, LANES), lax.all_gather(chip, "y_hi"))
     parts = lax.all_to_all(parts, "z", 0, 0, tiled=True)
     total = call(total_kernel, shape(HALF, LANES), parts)
@@ -201,7 +213,7 @@
 
 
 def solution(mesh):
-    fine = Mesh(mesh.devices.reshape(8, 2, 2, 4, 4), DP + GROUP)
+    fine = Mesh(mesh.devices.reshape(8, 2, 2, 2, 2, 4), DP + GROUP)
     rows = P(DP + GROUP)
     return jax.shard_map(
         on_device,

time: 90.5 us -> 83.2 us (0.919)
  blocking collectives: 71.5 us -> 47.6 us
  waiting for transfers between devices: 6.2 us -> 14.6 us
  starting transfers between devices: 4.52 us -> 12.7 us
    all_to_all x1 -> x0, blocking collectives: 35.4 us -> none  [on_device(): terms = lax.all_to_all(terms, GROUP, 0, 0, tiled=True)]
    all_gather x1 -> x2, blocking collectives: 4.63 us -> 16.1 us  [the longest x1 14.1 us: on_device(): got = lax.all_gather(send, 'y_mid')]
    all_to_all x1 -> x2, waiting for transfers between devices: 6.2 us -> 14.6 us  [the longest x1 9.3 us: on_device(): terms = lax.all_to_all(terms, ('y_low', 'x'), 0, 0, tiled=True)]
    all_to_all x1 -> x2, starting transfers between devices: 4.52 us -> 12.7 us  [the longest x1 6.82 us: on_device(): squares = lax.all_to_all(squares, ('core',) + GROUP, 0, 0, tiled=True)]
  transfers between devices with their start and end apart: 1 -> 2, of which waited for: 1 -> 2; matrix products, arithmetic and copies ran while one was open for 0% -> 0% of each run, Pallas kernels for 0% -> 0%
where the time goes in v3:
time: 83.2 us; the launch traced here: 82.9 us
  blocking collectives  47.6 us (57%)
  waiting for transfers between devices  14.6 us (18%)
  starting transfers between devices  12.7 us (15%)
  Pallas kernels  6 us (7%)
  between operations  1.34 us (2%)
    all_to_all x1, blocking collectives, on_device(): parts = lax.all_to_all(parts, 'z', 0, 0, tiled=True)  19.3 us
    all_gather x1, blocking collectives, on_device(): got = lax.all_gather(send, 'y_mid')  14.1 us
    all_to_all x1, waiting for transfers between devices, on_device(): terms = lax.all_to_all(terms, ('y_low', 'x'), 0, 0, tiled=True)  9.3 us
    all_gather x1, blocking collectives, on_device(): lax.all_gather(chip, 'y_hi')  7.35 us
    all_to_all x1, starting transfers between devices, on_device(): squares = lax.all_to_all(squares, ('core',) + GROUP, 0, 0, tiled=True)  6.82 us
    all_to_all x1, starting transfers between devices, on_device(): terms = lax.all_to_all(terms, ('y_low', 'x'), 0, 0, tiled=True)  5.88 us
    all_to_all x1, waiting for transfers between devices, on_device(): squares = lax.all_to_all(squares, ('core',) + GROUP, 0, 0, tiled=True)  5.32 us
    pallas_call x1, Pallas kernels, on_device(): pl.pallas_call(gradient_kernel, out_shape=shape(NEAR, SENT, LANES), in_sp...  5.03 us
  transfers between devices with their start and end apart: 2, of which 2 were waited for; matrix products, arithmetic and copies ran while one was open for 0% of the time, Pallas kernels for 0%

profile of v3, /device:TPU:1, one launch (start us, length us, event | category | flops | bytes accessed | tf_op | source)
XLA Modules:
  0.0 82.9 jit_solution(9865908752986838608)
XLA Ops:
  0.7 5.0 %shard_map.55 = f32[8,264,128]{2,1,0:T(8,128)} custom-call(bf16[256,4096]{1,0:T(8,128)(2,1)} %x_hbm.1, bf16[256,4096]{1,0:T(8,128)(2,1)} %c_hbm.1, bf16[2,2,16,4096]{3,2,1,0:T(8,128)(2,1)} %adapters_hbm.1, s32[1]{0:T(128)S(6)} %copy.7.user_ref), custom_call_target="tpu_custom_call" | custom-call | tf_op jit(solution)/shard_map/pallas_call | solution.py:183
  5.7 5.9 %all-to-all-start = ((f32[8,264,128]{2,1,0:T(8,128)}), f32[8,264,128]{2,1,0:T(8,128)S(1)}, u32[]{:S(2)}, u32[]{:S(2)}) async-start(f32[8,264,128]{2,1,0:T(8,128)} %shard_map.55), calls=%async_computation | async-start | bytes 2162688 | tf_op jit(solution)/shard_map/all_to_all | solution.py:198
  12.2 9.3 %all-to-all-done.got_ref = f32[8,264,128]{2,1,0:T(8,128)S(1)} async-done(((f32[8,264,128]{2,1,0:T(8,128)}), f32[8,264,128]{2,1,0:T(8,128)S(1)}, u32[]{:S(2)}, u32[]{:S(2)}) %all-to-all-start) | async-done | bytes 1081376 | tf_op jit(solution)/shard_map/all_to_all | solution.py:198
  21.5 0.2 shard_map.56
  21.7 14.1 %all-gather = f32[4,128,128]{2,1,0:T(8,128)S(1)} all-gather(f32[2,128,128]{2,1,0:T(8,128)S(1)} %get-tuple-element.10), channel_id=2, replica_groups=mesh['z'=8,'y_hi'=2,'core'=2,'y_mid'=2,'y_low'=2,'x'=4] {'y_mid'}, dimensions={0}, use_global_device_ids=true | all-gather | bytes 393216 | tf_op jit(solution)/shard_map/all_gather | solution.py:201
  35.7 0.7 shard_map.57
  36.5 6.8 %all-to-all-start.1 = ((f32[32,2,128]{2,1,0:T(2,128)}), f32[32,2,128]{2,1,0:T(2,128)S(1)}, u32[]{:S(2)}, u32[]{:S(2)}) async-start(f32[32,2,128]{2,1,0:T(2,128)} %get-tuple-element.11), calls=%async_computation.1 | async-start | bytes 65536 | tf_op jit(solution)/shard_map/all_to_all | solution.py:205
  43.3 2.0 %all-gather.1 = f32[4,128,128]{2,1,0:T(8,128)S(1)} all-gather(f32[2,128,128]{2,1,0:T(8,128)S(1)} %get-tuple-element.12), channel_id=3, replica_groups=mesh['z'=8,'y_hi'=2,'core'=2,'y_mid'=2,'y_low'=2,'x'=4] {'core'}, dimensions={0}, use_global_device_ids=true | all-gather | bytes 393216 | tf_op jit(solution)/shard_map/all_gather | solution.py:206
  45.3 5.3 %all-to-all-done.1.squares_ref = f32[32,2,128]{2,1,0:T(2,128)S(1)} async-done(((f32[32,2,128]{2,1,0:T(2,128)}), f32[32,2,128]{2,1,0:T(2,128)S(1)}, u32[]{:S(2)}, u32[]{:S(2)}) %all-to-all-start.1) | async-done | bytes 32800 | tf_op jit(solution)/shard_map/all_to_all | solution.py:205
  50.7 7.3 %all-gather.2 = f32[128,128]{1,0:T(8,128)S(1)} all-gather(f32[64,128]{1,0:T(8,128)S(1)} %shard_map.58), channel_id=4, replica_groups=mesh['z'=8,'y_hi'=2,'core'=2,'y_mid'=2,'y_low'=2,'x'=4] {'y_hi'}, dimensions={0}, use_global_device_ids=true | all-gather | bytes 98304 | tf_op jit(solution)/shard_map/all_gather | solution.py:208
  58.0 19.3 %all_to_all.15.parts_ref = f32[8,64,128]{2,1,0:T(8,128)S(1)} all-to-all(f32[8,64,128]{2,1,0:T(8,128)S(1)} %shard_map.59), channel_id=1, replica_groups=mesh['z'=8,'y_hi'=2,'core'=2,'y_mid'=2,'y_low'=2,'x'=4] {'z'}, dimensions={0} | all-to-all | bytes 524288 | tf_op jit(solution)/shard_map/all_to_all | solution.py:209
  77.4 4.9 %all_gather.27 = f32[64,256]{1,0:T(8,128)S(1)} all-gather(f32[64,128]{1,0:T(8,128)S(1)} %shard_map.60), channel_id=1, replica_groups=mesh['z'=8,'y_hi'=2,'core'=2,'y_mid'=2,'y_low'=2,'x'=4] {'core'}, dimensions={1}, use_global_device_ids=true | all-gather | bytes 98304 | tf_op jit(solution)/shard_map/all_gather | solution.py:211
  82.3 0.6 copy.9
  (3 shorter events, 0.1 us)
Async XLA Ops:
  5.7 15.8 %all-to-all-start = ((f32[8,264,128]{2,1,0:T(8,128)}), f32[8,264,128]{2,1,0:T(8,128)S(1)}, u32[]{:S(2)}, u32[]{:S(2)}) async-start(f32[8,264,128]{2,1,0:T(8,128)} %shard_map.55), calls=%async_computation | async-start | bytes 2162688 | tf_op jit(solution)/shard_map/all_to_all | solution.py:198
  36.5 14.1 %all-to-all-start.1 = ((f32[32,2,128]{2,1,0:T(2,128)}), f32[32,2,128]{2,1,0:T(2,128)S(1)}, u32[]{:S(2)}, u32[]{:S(2)}) async-start(f32[32,2,128]{2,1,0:T(2,128)} %get-tuple-element.11), calls=%async_computation.1 | async-start | bytes 65536 | tf_op jit(solution)/shard_map/all_to_all | solution.py:205

commit v4 on v3

--- a/solution.py
+++ b/solution.py
@@ -13,6 +13,7 @@
 WIDTH = 4096
 TOKENS = 256
 NEAR = 8
+NEAR_YS = 2
 FAR = 2
 PEERS = NEAR * FAR
 CORES = 2
@@ -23,7 +24,7 @@
 SENT = FAR * ROWS + 8
 USER_TOKENS = 8 * 256
 N_DP = 32
-PARTS = 4
+PARTS = 8
 PART = WIDTH // PARTS
 RING = 8
 
@@ -42,14 +43,12 @@
     return jax.ShapeDtypeStruct(dims, F32)
 
 
-def nt(a, b, precision=None):
-    return lax.dot_general(
-        a, b, (((1,), (1,)), ((), ())), preferred_element_type=F32, precision=precision
-    )
-
-
-def nn(a, b, precision=None):
-    return jnp.dot(a, b, preferred_element_type=F32, precision=precision)
+def nt(a, b):
+    return lax.dot_general(a, b, (((1,), (1,)), ((), ())), preferred_element_type=F32)
+
+
+def nn(a, b):
+    return jnp.dot(a, b, preferred_element_type=F32)
 
 
 def split(value):
@@ -91,11 +90,10 @@
         from_c += nt(jnp.concatenate([up2, up1], axis=0), c_ref[:, at])
         mixed += nt(down2, up1)
         mixed_t += nt(up1, down2)
-    exact = lax.Precision.HIGHEST
     z1 = from_x[:RANK].astype(BF16)
     q2 = from_c[:RANK].astype(BF16)
-    z2 = (from_x[RANK:] + SCALE * nn(mixed, z1.astype(F32), exact)).astype(BF16)
-    q1 = (from_c[RANK:] + SCALE * nn(mixed_t, q2.astype(F32), exact)).astype(BF16)
+    z2 = (from_x[RANK:] + halves(nn(split(SCALE * mixed), z1))).astype(BF16)
+    q1 = (from_c[RANK:] + halves(nn(split(SCALE * mixed_t), q2))).astype(BF16)
     cross = split((SCALE * SCALE) * nt(q2, z1))
     cross_t = split((SCALE * SCALE) * nt(z1, q2))
     left_x = jnp.concatenate([q1, q2], axis=0)
@@ -103,7 +101,7 @@
     sends = []
     for near in range(NEAR):
         for far in range(FAR):
-            columns = pl.ds((far * NEAR + near) * SLICE, SLICE)
+            columns = pl.ds((far * NEAR + near % NEAR_YS * (NEAR // NEAR_YS) + near // NEAR_YS) * SLICE, SLICE)
             to_x = SCALE * nn(left_x, x_ref[:, columns])
             to_c = SCALE * nn(left_c, c_ref[:, columns])
             add_a2 = halves(nn(cross, adapters_ref[0, 1, :, columns]))
@@ -195,7 +193,7 @@
         ],
         compiler_params=WIDE,
     )(activations, cotangent, adapters, user_ids)
-    terms = lax.all_to_all(terms, ("y_low", "x"), 0, 0, tiled=True)
+    terms = lax.all_to_all(terms, ("x", "y_low"), 0, 0, tiled=True)
     users = shape(GROUP_USERS, ROWS, LANES)
     keep, send = call(users_kernel, (users, users), mid, terms, scalars=1)
     got = lax.all_gather(send, "y_mid")

time: 83.2 us -> 82.7 us (level)
  blocking collectives: 47.6 us -> 43.7 us
  starting transfers between devices: 12.7 us -> 15 us
  waiting for transfers between devices: 14.6 us -> 16 us
    all_gather x1, blocking collectives: 14.1 us -> 10.2 us  [on_device(): got = lax.all_gather(send, 'y_mid')]
    all_to_all x1, starting transfers between devices: 6.82 us -> 9.08 us  [on_device(): squares = lax.all_to_all(squares, ('core',) + GROUP, 0, 0, tiled=True)]
    all_to_all x1, waiting for transfers between devices: 9.3 us -> 10.7 us  [on_device(): terms = lax.all_to_all(terms, ('x', 'y_low'), 0, 0, tiled=True)]
where the time goes in v4:
time: 82.7 us; the launch traced here: 82.4 us
  blocking collectives  43.7 us (53%)
  waiting for transfers between devices  16 us (19%)
  starting transfers between devices  15 us (18%)
  Pallas kernels  5.73 us (7%)
  between operations  1.34 us (2%)
    all_to_all x1, blocking collectives, on_device(): parts = lax.all_to_all(parts, 'z', 0, 0, tiled=True)  19.2 us
    all_to_all x1, waiting for transfers between devices, on_device(): terms = lax.all_to_all(terms, ('x', 'y_low'), 0, 0, tiled=True)  10.7 us
    all_gather x1, blocking collectives, on_device(): got = lax.all_gather(send, 'y_mid')  10.2 us
    all_to_all x1, starting transfers between devices, on_device(): squares = lax.all_to_all(squares, ('core',) + GROUP, 0, 0, tiled=True)  9.08 us
    all_gather x1, blocking collectives, on_device(): lax.all_gather(chip, 'y_hi')  7.35 us
    all_to_all x1, starting transfers between devices, on_device(): terms = lax.all_to_all(terms, ('x', 'y_low'), 0, 0, tiled=True)  5.88 us
    all_to_all x1, waiting for transfers between devices, on_device(): squares = lax.all_to_all(squares, ('core',) + GROUP, 0, 0, tiled=True)  5.32 us
    all_gather x1, blocking collectives, on_device(): total = lax.all_gather(total, 'core', axis=1, tiled=True)  4.94 us
  transfers between devices with their start and end apart: 2, of which 2 were waited for; matrix products, arithmetic and copies ran while one was open for 0% of the time, Pallas kernels for 0%

profile of v4, /device:TPU:1, one launch (start us, length us, event | category | flops | bytes accessed | tf_op | source)
XLA Modules:
  0.0 82.4 jit_solution(17262830120383794620)
XLA Ops:
  0.7 4.8 %shard_map.55 = f32[8,264,128]{2,1,0:T(8,128)} custom-call(bf16[256,4096]{1,0:T(8,128)(2,1)} %x_hbm.1, bf16[256,4096]{1,0:T(8,128)(2,1)} %c_hbm.1, bf16[2,2,16,4096]{3,2,1,0:T(8,128)(2,1)} %adapters_hbm.1, s32[1]{0:T(128)S(6)} %copy.7.user_ref), custom_call_target="tpu_custom_call" | custom-call | tf_op jit(solution)/shard_map/pallas_call | solution.py:181
  5.4 5.9 %all-to-all-start = ((f32[8,264,128]{2,1,0:T(8,128)}), f32[8,264,128]{2,1,0:T(8,128)S(1)}, u32[]{:S(2)}, u32[]{:S(2)}) async-start(f32[8,264,128]{2,1,0:T(8,128)} %shard_map.55), calls=%async_computation | async-start | bytes 2162688 | tf_op jit(solution)/shard_map/all_to_all | solution.py:196
  11.9 10.7 %all-to-all-done.got_ref = f32[8,264,128]{2,1,0:T(8,128)S(1)} async-done(((f32[8,264,128]{2,1,0:T(8,128)}), f32[8,264,128]{2,1,0:T(8,128)S(1)}, u32[]{:S(2)}, u32[]{:S(2)}) %all-to-all-start) | async-done | bytes 1081376 | tf_op jit(solution)/shard_map/all_to_all | solution.py:196
  22.7 0.2 shard_map.56
  22.8 10.2 %all-gather = f32[4,128,128]{2,1,0:T(8,128)S(1)} all-gather(f32[2,128,128]{2,1,0:T(8,128)S(1)} %get-tuple-element.10), channel_id=2, replica_groups=mesh['z'=8,'y_hi'=2,'core'=2,'y_mid'=2,'y_low'=2,'x'=4] {'y_mid'}, dimensions={0}, use_global_device_ids=true | all-gather | bytes 393216 | tf_op jit(solution)/shard_map/all_gather | solution.py:199
  33.0 0.7 shard_map.57
  33.8 9.1 %all-to-all-start.1 = ((f32[32,2,128]{2,1,0:T(2,128)}), f32[32,2,128]{2,1,0:T(2,128)S(1)}, u32[]{:S(2)}, u32[]{:S(2)}) async-start(f32[32,2,128]{2,1,0:T(2,128)} %get-tuple-element.11), calls=%async_computation.1 | async-start | bytes 65536 | tf_op jit(solution)/shard_map/all_to_all | solution.py:203
  42.9 2.0 %all-gather.1 = f32[4,128,128]{2,1,0:T(8,128)S(1)} all-gather(f32[2,128,128]{2,1,0:T(8,128)S(1)} %get-tuple-element.12), channel_id=3, replica_groups=mesh['z'=8,'y_hi'=2,'core'=2,'y_mid'=2,'y_low'=2,'x'=4] {'core'}, dimensions={0}, use_global_device_ids=true | all-gather | bytes 393216 | tf_op jit(solution)/shard_map/all_gather | solution.py:204
  44.8 5.3 %all-to-all-done.1.squares_ref = f32[32,2,128]{2,1,0:T(2,128)S(1)} async-done(((f32[32,2,128]{2,1,0:T(2,128)}), f32[32,2,128]{2,1,0:T(2,128)S(1)}, u32[]{:S(2)}, u32[]{:S(2)}) %all-to-all-start.1) | async-done | bytes 32800 | tf_op jit(solution)/shard_map/all_to_all | solution.py:203
  50.2 7.3 %all-gather.2 = f32[128,128]{1,0:T(8,128)S(1)} all-gather(f32[64,128]{1,0:T(8,128)S(1)} %shard_map.58), channel_id=4, replica_groups=mesh['z'=8,'y_hi'=2,'core'=2,'y_mid'=2,'y_low'=2,'x'=4] {'y_hi'}, dimensions={0}, use_global_device_ids=true | all-gather | bytes 98304 | tf_op jit(solution)/shard_map/all_gather | solution.py:206
  57.6 19.2 %all_to_all.15.parts_ref = f32[8,64,128]{2,1,0:T(8,128)S(1)} all-to-all(f32[8,64,128]{2,1,0:T(8,128)S(1)} %shard_map.59), channel_id=1, replica_groups=mesh['z'=8,'y_hi'=2,'core'=2,'y_mid'=2,'y_low'=2,'x'=4] {'z'}, dimensions={0} | all-to-all | bytes 524288 | tf_op jit(solution)/shard_map/all_to_all | solution.py:207
  76.8 4.9 %all_gather.27 = f32[64,256]{1,0:T(8,128)S(1)} all-gather(f32[64,128]{1,0:T(8,128)S(1)} %shard_map.60), channel_id=1, replica_groups=mesh['z'=8,'y_hi'=2,'core'=2,'y_mid'=2,'y_low'=2,'x'=4] {'core'}, dimensions={1}, use_global_device_ids=true | all-gather | bytes 98304 | tf_op jit(solution)/shard_map/all_gather | solution.py:209
  81.8 0.6 copy.9
  (3 shorter events, 0.1 us)
Async XLA Ops:
  5.4 17.2 %all-to-all-start = ((f32[8,264,128]{2,1,0:T(8,128)}), f32[8,264,128]{2,1,0:T(8,128)S(1)}, u32[]{:S(2)}, u32[]{:S(2)}) async-start(f32[8,264,128]{2,1,0:T(8,128)} %shard_map.55), calls=%async_computation | async-start | bytes 2162688 | tf_op jit(solution)/shard_map/all_to_all | solution.py:196
  33.8 16.4 %all-to-all-start.1 = ((f32[32,2,128]{2,1,0:T(2,128)}), f32[32,2,128]{2,1,0:T(2,128)S(1)}, u32[]{:S(2)}, u32[]{:S(2)}) async-start(f32[32,2,128]{2,1,0:T(2,128)} %get-tuple-element.11), calls=%async_computation.1 | async-start | bytes 65536 | tf_op jit(solution)/shard_map/all_to_all | solution.py:203

commit v5 on v4

--- a/solution.py
+++ b/solution.py
@@ -193,6 +193,7 @@
         ],
         compiler_params=WIDE,
     )(activations, cotangent, adapters, user_ids)
+    terms, mid, core, clip_norm_ratio = lax.optimization_barrier((terms, mid, core, clip_norm_ratio))
     terms = lax.all_to_all(terms, ("x", "y_low"), 0, 0, tiled=True)
     users = shape(GROUP_USERS, ROWS, LANES)
     keep, send = call(users_kernel, (users, users), mid, terms, scalars=1)

time: 82.7 us -> 82.7 us (level)
  no operation moved by 1% of the time
where the time goes in v5:
time: 82.7 us; the launch traced here: 82.4 us
  blocking collectives  43.7 us (53%)
  waiting for transfers between devices  16 us (19%)
  starting transfers between devices  15 us (18%)
  Pallas kernels  5.73 us (7%)
  between operations  1.34 us (2%)
    all_to_all x1, blocking collectives, on_device(): parts = lax.all_to_all(parts, 'z', 0, 0, tiled=True)  19.2 us
    all_to_all x1, waiting for transfers between devices, on_device(): terms = lax.all_to_all(terms, ('x', 'y_low'), 0, 0, tiled=True)  10.7 us
    all_gather x1, blocking collectives, on_device(): got = lax.all_gather(send, 'y_mid')  10.2 us
    all_to_all x1, starting transfers between devices, on_device(): squares = lax.all_to_all(squares, ('core',) + GROUP, 0, 0, tiled=True)  9.08 us
    all_gather x1, blocking collectives, on_device(): lax.all_gather(chip, 'y_hi')  7.35 us
    all_to_all x1, starting transfers between devices, on_device(): terms = lax.all_to_all(terms, ('x', 'y_low'), 0, 0, tiled=True)  5.88 us
    all_to_all x1, waiting for transfers between devices, on_device(): squares = lax.all_to_all(squares, ('core',) + GROUP, 0, 0, tiled=True)  5.32 us
    all_gather x1, blocking collectives, on_device(): total = lax.all_gather(total, 'core', axis=1, tiled=True)  4.94 us
  transfers between devices with their start and end apart: 2, of which 2 were waited for; matrix products, arithmetic and copies ran while one was open for 0% of the time, Pallas kernels for 0%

profile of v5, /device:TPU:1, one launch (start us, length us, event | category | flops | bytes accessed | tf_op | source)
XLA Modules:
  0.0 82.4 jit_solution(16877910804387437340)
XLA Ops:
  0.7 4.8 %shard_map.55 = f32[8,264,128]{2,1,0:T(8,128)} custom-call(bf16[256,4096]{1,0:T(8,128)(2,1)} %x_hbm.1, bf16[256,4096]{1,0:T(8,128)(2,1)} %c_hbm.1, bf16[2,2,16,4096]{3,2,1,0:T(8,128)(2,1)} %adapters_hbm.1, s32[1]{0:T(128)S(6)} %copy.7.user_ref), custom_call_target="tpu_custom_call" | custom-call | tf_op jit(solution)/shard_map/pallas_call | solution.py:181
  5.4 5.9 %all-to-all-start = ((f32[8,264,128]{2,1,0:T(8,128)}), f32[8,264,128]{2,1,0:T(8,128)S(1)}, u32[]{:S(2)}, u32[]{:S(2)}) async-start(f32[8,264,128]{2,1,0:T(8,128)} %shard_map.55), calls=%async_computation | async-start | bytes 2162688 | tf_op jit(solution)/shard_map/all_to_all | solution.py:197
  11.9 10.7 %all-to-all-done.got_ref = f32[8,264,128]{2,1,0:T(8,128)S(1)} async-done(((f32[8,264,128]{2,1,0:T(8,128)}), f32[8,264,128]{2,1,0:T(8,128)S(1)}, u32[]{:S(2)}, u32[]{:S(2)}) %all-to-all-start) | async-done | bytes 1081376 | tf_op jit(solution)/shard_map/all_to_all | solution.py:197
  22.7 0.2 shard_map.56
  22.8 10.2 %all-gather = f32[4,128,128]{2,1,0:T(8,128)S(1)} all-gather(f32[2,128,128]{2,1,0:T(8,128)S(1)} %get-tuple-element.18), channel_id=2, replica_groups=mesh['z'=8,'y_hi'=2,'core'=2,'y_mid'=2,'y_low'=2,'x'=4] {'y_mid'}, dimensions={0}, use_global_device_ids=true | all-gather | bytes 393216 | tf_op jit(solution)/shard_map/all_gather | solution.py:200
  33.0 0.7 shard_map.57
  33.8 9.1 %all-to-all-start.1 = ((f32[32,2,128]{2,1,0:T(2,128)}), f32[32,2,128]{2,1,0:T(2,128)S(1)}, u32[]{:S(2)}, u32[]{:S(2)}) async-start(f32[32,2,128]{2,1,0:T(2,128)} %get-tuple-element.19), calls=%async_computation.1 | async-start | bytes 65536 | tf_op jit(solution)/shard_map/all_to_all | solution.py:204
  42.9 2.0 %all-gather.1 = f32[4,128,128]{2,1,0:T(8,128)S(1)} all-gather(f32[2,128,128]{2,1,0:T(8,128)S(1)} %get-tuple-element.20), channel_id=3, replica_groups=mesh['z'=8,'y_hi'=2,'core'=2,'y_mid'=2,'y_low'=2,'x'=4] {'core'}, dimensions={0}, use_global_device_ids=true | all-gather | bytes 393216 | tf_op jit(solution)/shard_map/all_gather | solution.py:205
  44.8 5.3 %all-to-all-done.1.squares_ref = f32[32,2,128]{2,1,0:T(2,128)S(1)} async-done(((f32[32,2,128]{2,1,0:T(2,128)}), f32[32,2,128]{2,1,0:T(2,128)S(1)}, u32[]{:S(2)}, u32[]{:S(2)}) %all-to-all-start.1) | async-done | bytes 32800 | tf_op jit(solution)/shard_map/all_to_all | solution.py:204
  50.2 7.3 %all-gather.2 = f32[128,128]{1,0:T(8,128)S(1)} all-gather(f32[64,128]{1,0:T(8,128)S(1)} %shard_map.58), channel_id=4, replica_groups=mesh['z'=8,'y_hi'=2,'core'=2,'y_mid'=2,'y_low'=2,'x'=4] {'y_hi'}, dimensions={0}, use_global_device_ids=true | all-gather | bytes 98304 | tf_op jit(solution)/shard_map/all_gather | solution.py:207
  57.6 19.2 %all_to_all.15.parts_ref = f32[8,64,128]{2,1,0:T(8,128)S(1)} all-to-all(f32[8,64,128]{2,1,0:T(8,128)S(1)} %shard_map.59), channel_id=1, replica_groups=mesh['z'=8,'y_hi'=2,'core'=2,'y_mid'=2,'y_low'=2,'x'=4] {'z'}, dimensions={0} | all-to-all | bytes 524288 | tf_op jit(solution)/shard_map/all_to_all | solution.py:208
  76.8 4.9 %all_gather.27 = f32[64,256]{1,0:T(8,128)S(1)} all-gather(f32[64,128]{1,0:T(8,128)S(1)} %shard_map.60), channel_id=1, replica_groups=mesh['z'=8,'y_hi'=2,'core'=2,'y_mid'=2,'y_low'=2,'x'=4] {'core'}, dimensions={1}, use_global_device_ids=true | all-gather | bytes 98304 | tf_op jit(solution)/shard_map/all_gather | solution.py:210
  81.8 0.6 copy.9
  (3 shorter events, 0.1 us)
Async XLA Ops:
  5.4 17.2 %all-to-all-start = ((f32[8,264,128]{2,1,0:T(8,128)}), f32[8,264,128]{2,1,0:T(8,128)S(1)}, u32[]{:S(2)}, u32[]{:S(2)}) async-start(f32[8,264,128]{2,1,0:T(8,128)} %shard_map.55), calls=%async_computation | async-start | bytes 2162688 | tf_op jit(solution)/shard_map/all_to_all | solution.py:197
  33.8 16.4 %all-to-all-start.1 = ((f32[32,2,128]{2,1,0:T(2,128)}), f32[32,2,128]{2,1,0:T(2,128)S(1)}, u32[]{:S(2)}, u32[]{:S(2)}) async-start(f32[32,2,128]{2,1,0:T(2,128)} %get-tuple-element.19), calls=%async_computation.1 | async-start | bytes 65536 | tf_op jit(solution)/shard_map/all_to_all | solution.py:204
